TPU v7x, 32 devices: a whole 2x2x4 slice. The times are simulated.
32 devices in a mesh: date: 8 (over z, x), space: 4 (over y, core).
Axes of the slice: x: 2, y: 2, z: 4, core: 2. Of those that a mesh axis runs over, the one named last changes fastest.
Arguments:
- frames: bfloat16 [32, 1024, 1024], P('date', 'space'), may hold values from -6 to 6
- cloud_mask: int32 [32, 1024], P('date', 'space'), may hold values from 0 to 1
- qkv_weight: bfloat16 [2, 1024, 3072], replicated, may hold values from -0.1875 to 0.1875
- out_weight: bfloat16 [2, 1024, 1024], replicated, may hold values from -0.1875 to 0.1875
- norm_gain: float32 [2, 1024], replicated, may hold values from 0.1 to 1.9
- head_norm_scale: float32 [2, 1024], replicated, may hold values from 0.1 to 1.9
- decay: float32 [2, 32, 16], P(None, 'date'), as said below
Outputs:
- forecast: bfloat16 [32, 1024, 1024], P('date', 'space')
Inputs may be any that keep to these rules, and one draw needn't show every extreme that they name: `decay`: every entry lies strictly between 0 and 1.
All inputs are finite; a program needn't handle non-finite values.
Results may differ from a plain program's by a relative error of at most 0.0065.
Values may be sent and summed in bfloat16 or wider, within the bound.
A program may use at most 128 MiB of HBM per device.

v0:
```python
import jax
import jax.numpy as jnp
from jax import lax
from jax.sharding import PartitionSpec as P

HEADS = 16
HEAD = 64
STACK_LEVELS = 2


def carried_in(value, axis, join, neutral):
    count, mine = (lax.axis_size(axis), lax.axis_index(axis))
    pieces = jax.tree.map(lambda part: lax.all_gather(part, axis), value)
    subtotal = jax.tree.map(
        lambda part, zero: jnp.full_like(part, 0) + jnp.asarray(zero, part.dtype), value, neutral
    )

    def step(position, subtotal):
        longer = join(subtotal, jax.tree.map(lambda part: part[position], pieces))
        return jax.tree.map(lambda new, old: jnp.where(position < mine, new, old), longer, subtotal)

    return lax.fori_loop(0, count - 1, step, subtotal)


def feature(u):
    return jax.nn.elu(u) + 1.0


def chain(earlier, later):
    return (earlier[0] * later[1][:, None, None] + later[0], earlier[1] * later[1])


def shards(frames, cloud_mask, qkv_weight, out_weight, norm_gain, head_norm_scale, decay):
    dates_here, tokens_here, width = frames.shape
    heads = HEADS
    current = frames
    flag_f = cloud_mask.astype(jnp.float32)[:, :, None]
    for layer in range(STACK_LEVELS):
        xf = current.astype(jnp.float32)
        in_msq = jnp.mean(xf * xf, -1, keepdims=True) + 1e-05
        normalized_output = (xf * lax.rsqrt(in_msq) * norm_gain[layer]).astype(jnp.bfloat16)
        proj = jnp.dot(
            normalized_output.reshape(-1, width),
            qkv_weight[layer],
            preferred_element_type=jnp.float32,
        )
        proj = proj.reshape(dates_here, tokens_here, 3 * width)
        query = (
            feature(proj[:, :, :width])
            .astype(jnp.bfloat16)
            .reshape(dates_here, tokens_here, heads, HEAD)
        )
        key = (
            (feature(proj[:, :, width : 2 * width]) * flag_f)
            .astype(jnp.bfloat16)
            .reshape(dates_here, tokens_here, heads, HEAD)
        )
        value = (
            proj[:, :, 2 * width :]
            .astype(jnp.bfloat16)
            .reshape(dates_here, tokens_here, heads, HEAD)
        )
        pairing_partial = jnp.einsum(
            "tshe,tshf->thef", key, value, preferred_element_type=jnp.float32
        )
        kv = lax.psum(pairing_partial, "space")
        persist_factor = decay[layer]

        def advance(state, inputs):
            state = inputs[1][:, None, None] * state + inputs[0]
            return (state, state)

        start = jnp.zeros((heads, HEAD, HEAD), jnp.float32)
        last_state, local_states = lax.scan(advance, start, (kv, persist_factor))
        kept = jnp.cumprod(persist_factor, axis=0)
        total_kept = kept[-1]
        incoming, _ = carried_in(
            (last_state, total_kept),
            "date",
            chain,
            (jnp.zeros_like(last_state), jnp.ones_like(total_kept)),
        )
        states = local_states + kept[:, :, None, None] * incoming[None]
        state_b = states.astype(jnp.bfloat16)
        numer = jnp.einsum("tshe,thef->tshf", query, state_b, preferred_element_type=jnp.float32)
        head_msq = jnp.mean(numer * numer, -1, keepdims=True) + 1e-05
        numer = numer * lax.rsqrt(head_msq)
        mixed = (numer.reshape(dates_here, tokens_here, width) * head_norm_scale[layer]).astype(
            jnp.bfloat16
        )
        update = jnp.dot(
            mixed.reshape(-1, width), out_weight[layer], preferred_element_type=jnp.float32
        )
        current = (xf + update.reshape(dates_here, tokens_here, width)).astype(jnp.bfloat16)
    return current


def solution(mesh):
    placed = (
        P("date", "space", None),
        P("date", "space"),
        P(),
        P(),
        P(),
        P(),
        P(None, "date", None),
    )
    return jax.shard_map(
        shards, mesh=mesh, in_specs=placed, out_specs=P("date", "space", None), check_vma=False
    )
```

profile of v0, /device:TPU:0, one launch (start us, length us, event | category | flops | bytes accessed | tf_op | source)
XLA Modules:
  0.0 362.9 jit_solution(13687591344482895535)
XLA Ops:
  9.5 8.9 %fusion.6 = f32[4,256,3072]{2,1,0:T(8,128)S(1)} fusion(bf16[2,1024,3072]{2,1,0:T(8,128)(2,1)} %param.17, bf16[4,256,1024]{2,1,0:T(8,128)(2,1)S(1)} %copy-done.4, f32[1024]{0:T(1024)S(1)} %bitcast.125, f32[4,256]{1,0:T(4,128)S(1)} %add_rsqrt_fusion.3), kind=kOutput, calls=%fused_computation.26 | convolution fusion | flops 6446645248 | bytes 20979712 | tf_op jit(solution)/shard_map/dot_general | solution.py:42
  20.1 5.1 %fusion.21 = (bf16[4,256,1024]{2,1,0:T(8,128)(2,1)}, bf16[4,256,1024]{2,1,0:T(8,128)(2,1)}) fusion(f32[4,256,3072]{2,1,0:T(8,128)S(1)} %fusion.6, f32[4,256]{1,0:T(4,128)S(1)} %convert_element_type.59), kind=kLoop, calls=%fused_computation.47 | loop fusion | flops 11534336 | bytes 12587008 | tf_op jit(solution)/shard_map/convert_element_type | solution.py:55
  25.2 2.8 copy.28
  28.0 3.9 %copy.29 = bf16[4,256,1024]{1,2,0:T(8,128)(2,1)} copy(bf16[4,256,1024]{2,1,0:T(8,128)(2,1)} %slice.113) | data formatting | bytes 4194304 | tf_op jit(solution)/shard_map/slice | solution.py:59
  32.0 3.6 fusion.61
  36.3 53.6 %all-reduce.3.cloned.1.call-done = f32[4,16,64,64]{3,2,1,0:T(8,128)} async-done(((f32[4,16,64,64]{3,2,1,0:T(8,128)}), f32[4,16,64,64]{3,2,1,0:T(8,128)}) %all-reduce.3.cloned.1.call-update) | async-done | bytes 1048592 | tf_op jit(solution)/shard_map/psum | solution.py:66
  90.1 4.9 %while.54 = (s32[]{:T(128)}, f32[16,64,64]{2,1,0:T(8,128)S(1)}, f32[4,16,64,64]{3,2,1,0:T(8,128)S(1)}, f32[4,16]{1,0:T(4,128)S(1)}, f32[4,16,64,64]{3,2,1,0:T(8,128)}, /*index=5*/s32[]{:T(128)}, s32[]{:T(128)}) while((s32[]{:T(128)}, f32[16,64,64]{2,1,0:T(8,128)S(1)}, f32[4,16,64,64]{3,2,1,0:T(8,128)S(1)}, f32[4,16]{1,0:T(4,128)S(1)}, ...), condition=%wide.region_3.4_spmd.clone, body=%wide.region_2.3_spmd.clone.sunk | while | flops 196611 | bytes 1835743 | solution.py:74
  96.5 2.9 copy.30
  99.5 20.8 %all-gather.2 = f32[8,1,16]{2,1,0:T(1,128)S(1)} all-gather(f32[1,1,16]{2,1,0:T(1,128)S(1)} %slice_bitcast_fusion.3), channel_id=1, replica_groups=mesh['date'=8,'space'=4] {'date'}, dimensions={0}, use_global_device_ids=true | all-gather | bytes 576 | tf_op jit(solution)/shard_map/all_gather | solution.py:13
  120.3 49.2 %all-gather.7.cloned.1.call-done = f32[128,64,64]{2,1,0:T(8,128)} async-done(((f32[16,64,64]{2,1,0:T(8,128)}), f32[128,64,64]{2,1,0:T(8,128)}) %all-gather.7.cloned.1.call-update) | async-done | bytes 2097168 | tf_op jit(solution)/shard_map/all_gather | solution.py:13
  169.4 8.4 %while.55 = (s32[]{:T(128)}, f32[16,64,64]{2,1,0:T(8,128)S(1)}, s32[]{:T(128)}, f32[8,16]{1,0:T(8,128)S(1)}, f32[8,16,64,64]{3,2,1,0:T(8,128)}, /*index=5*/s32[]{:T(128)}, s32[]{:T(128)}) while((s32[]{:T(128)}, f32[16,64,64]{2,1,0:T(8,128)S(1)}, s32[]{:T(128)}, f32[8,16]{1,0:T(8,128)S(1)}, f32[8,16,64,64]{3,2,1,0:T(8,128)}, ...), condition=%wide.region_6.7_spmd.clone, body=%wide.region_5.6_spmd.clone.sunk | while | flops 262148 | bytes 786729 | solution.py:22
  177.9 2.7 fusion.35
  185.4 6.7 %fusion.4 = f32[4,256,3072]{2,1,0:T(8,128)S(1)} fusion(bf16[2,1024,3072]{2,1,0:T(8,128)(2,1)S(1)} %bitcast.127, bf16[4,256,1024]{2,1,0:T(8,128)(2,1)S(1)} %get-tuple-element.384, f32[1024]{0:T(1024)S(1)} %bitcast.124, f32[4,256]{1,0:T(4,128)S(1)} %add_rsqrt_fusion.2), kind=kOutput, calls=%fused_computation.24 | convolution fusion | flops 6446645248 | bytes 20979712 | tf_op jit(solution)/shard_map/dot_general | solution.py:42
  192.1 5.1 %fusion.28 = (bf16[4,256,1024]{2,1,0:T(8,128)(2,1)}, bf16[4,256,1024]{2,1,0:T(8,128)(2,1)}) fusion(f32[4,256,3072]{2,1,0:T(8,128)S(1)} %fusion.4, f32[4,256]{1,0:T(4,128)S(1)} %convert_element_type.59), kind=kLoop, calls=%fused_computation.54 | loop fusion | flops 11534336 | bytes 12587008 | tf_op jit(solution)/shard_map/convert_element_type | solution.py:55
  198.8 2.8 copy.33
  201.7 3.9 %copy.34 = bf16[4,256,1024]{1,2,0:T(8,128)(2,1)} copy(bf16[4,256,1024]{2,1,0:T(8,128)(2,1)} %slice.112) | data formatting | bytes 4194304 | tf_op jit(solution)/shard_map/slice | solution.py:59
  205.6 3.6 fusion.62
  209.5 49.5 %all-reduce.5.cloned.1.call-done = f32[4,16,64,64]{3,2,1,0:T(8,128)} async-done(((f32[4,16,64,64]{3,2,1,0:T(8,128)}), f32[4,16,64,64]{3,2,1,0:T(8,128)}) %all-reduce.5.cloned.1.call-update) | async-done | bytes 1048592 | tf_op jit(solution)/shard_map/psum | solution.py:66
  259.3 4.9 %while.56 = (s32[]{:T(128)}, f32[16,64,64]{2,1,0:T(8,128)S(1)}, f32[4,16,64,64]{3,2,1,0:T(8,128)S(1)}, f32[4,16]{1,0:T(4,128)S(1)}, f32[4,16,64,64]{3,2,1,0:T(8,128)}, /*index=5*/s32[]{:T(128)}, s32[]{:T(128)}) while((s32[]{:T(128)}, f32[16,64,64]{2,1,0:T(8,128)S(1)}, f32[4,16,64,64]{3,2,1,0:T(8,128)S(1)}, ...), condition=%wide.region_11.12_spmd.clone, body=%wide.region_10.11_spmd.clone.sunk | while | flops 196611 | bytes 1835743 | solution.py:74
  265.2 20.5 %all-gather.3 = f32[8,1,16]{2,1,0:T(1,128)S(1)} all-gather(f32[1,1,16]{2,1,0:T(1,128)S(1)} %slice_bitcast_fusion.2), channel_id=1, replica_groups=mesh['date'=8,'space'=4] {'date'}, dimensions={0}, use_global_device_ids=true | all-gather | bytes 576 | tf_op jit(solution)/shard_map/all_gather | solution.py:13
  285.7 2.8 copy.35
  288.5 50.2 %all-gather.9.cloned.1.call-done = f32[128,64,64]{2,1,0:T(8,128)} async-done(((f32[16,64,64]{2,1,0:T(8,128)}), f32[128,64,64]{2,1,0:T(8,128)}) %all-gather.9.cloned.1.call-update) | async-done | bytes 2097168 | tf_op jit(solution)/shard_map/all_gather | solution.py:13
  338.7 8.4 %while.57 = (s32[]{:T(128)}, f32[16,64,64]{2,1,0:T(8,128)S(1)}, s32[]{:T(128)}, f32[8,16]{1,0:T(8,128)S(1)}, f32[8,16,64,64]{3,2,1,0:T(8,128)}, /*index=5*/s32[]{:T(128)}, s32[]{:T(128)}) while((s32[]{:T(128)}, f32[16,64,64]{2,1,0:T(8,128)S(1)}, s32[]{:T(128)}, f32[8,16]{1,0:T(8,128)S(1)}, f32[8,16,64,64]{3,2,1,0:T(8,128)}, ...), condition=%wide.region_14.15_spmd.clone, body=%wide.region_13.14_spmd.clone.sunk | while | flops 262148 | bytes 786729 | solution.py:22
  352.6 3.7 %fusion.17 = bf16[4,256,1024]{2,1,0:T(8,128)(2,1)} fusion(bf16[4,256,1024]{2,1,0:T(8,128)(2,1)S(1)} %copy-done.12, bf16[4,256,1024]{1,2,0:T(8,128)(2,1)S(1)} %bitcast.119, bf16[2,1024,1024]{2,1,0:T(8,128)(2,1)S(1)} %copy-done.10), kind=kOutput, calls=%fused_computation.43 | convolution fusion | flops 2150629376 | bytes 8388608 | tf_op jit(solution)/shard_map/dot_general | solution.py:91
  (112 shorter events, 46.3 us)
Async XLA Ops:
  6.5 3.0 copy-start.4
  6.5 3.0 copy-start.7
  6.5 83.3 %all-reduce.3.cloned.1.call-start = ((), (), s32[]{:S(2)}) async-start(), calls=%async_computation | async-start | bytes 4194304 | tf_op jit(solution)/shard_map/psum | solution.py:66
  35.6 0.7 copy-start.8
  35.6 133.8 %all-gather.7.cloned.1.call-start = ((), (), s32[]{:S(2)}) async-start(), calls=%async_computation.2 | async-start | bytes 4718592 | tf_op jit(solution)/shard_map/all_gather | solution.py:13
  95.0 0.8 copy-start
  95.0 1.5 copy-start.3
  95.8 163.3 %all-reduce.5.cloned.1.call-start = ((), (), s32[]{:S(2)}) async-start(), calls=%async_computation.1 | async-start | bytes 4194304 | tf_op jit(solution)/shard_map/psum | solution.py:66
  96.5 2.9 copy-start.6
  177.9 3.3 copy-start.9
  177.9 7.4 %slice-start = ((s8[12582912]{0:T(1024)(128)(4,1)}), s8[4194304]{0:T(1024)(128)(4,1)S(1)}, s32[]{:S(2)}) async-start(s8[12582912]{0:T(1024)(128)(4,1)} %bitcast.126), calls=%async_computation.4 | async-start | bytes 8388608
  180.7 1.9 copy-start.5
  180.7 4.6 %slice-start.1 = ((s8[12582912]{0:T(1024)(128)(4,1)}), s8[4194304]{0:T(1024)(128)(4,1)S(1)}, s32[]{:S(2)}) async-start(s8[12582912]{0:T(1024)(128)(4,1)} %bitcast.126), calls=%async_computation.5 | async-start | bytes 8388608
  182.6 2.8 slice-start.2
  185.3 6.8 %copy-start.11 = (bf16[4,256,1024]{2,1,0:T(8,128)(2,1)}, bf16[4,256,1024]{2,1,0:T(8,128)(2,1)S(1)}, u32[]{:S(2)}) copy-start(bf16[4,256,1024]{2,1,0:T(8,128)(2,1)S(1)} %get-tuple-element.384) | copy-start | bytes 6291460
  209.3 129.5 %all-gather.9.cloned.1.call-start = ((), (), s32[]{:S(2)}) async-start(), calls=%async_computation.3 | async-start | bytes 4718592 | tf_op jit(solution)/shard_map/all_gather | solution.py:13
  264.2 0.8 copy-start.1
  264.2 21.5 %copy-start.2 = (f32[4,16,64,64]{3,2,1,0:T(8,128)}, f32[4,16,64,64]{3,2,1,0:T(8,128)S(1)}, u32[]{:S(2)}) copy-start(f32[4,16,64,64]{3,2,1,0:T(8,128)S(1)} %get-tuple-element.252) | copy-start | bytes 3145732
  349.8 2.2 copy-start.10
  349.8 2.9 copy-start.12
Sparse Core Ops, SparseCore 0:
  35.7 54.0 all-reduce.2
  95.9 73.4 all-gather.6
  209.4 49.6 all-reduce.4
  265.2 73.4 all-gather.8
where the time goes:
time: 365 us; the launch traced here: 363 us
  waiting for transfers between devices  203 us (56%)
  blocking collectives  41.3 us (11%)
  other arithmetic  39.3 us (11%)
  matrix products  34.5 us (9%)
  local copies, waits for them, and re-layouts  30.8 us (8%)
  between operations  13.5 us (4%)
    psum x2, waiting for transfers between devices, shards(): kv = lax.psum(pairing_partial, 'space')  103 us
    all_gather x2, waiting for transfers between devices, carried_in(): pieces = jax.tree.map(lambda part: lax.all_gather(part, axis), value)  99.3 us
    all_gather x2, blocking collectives, carried_in(): pieces = jax.tree.map(lambda part: lax.all_gather(part, axis), value)  41.3 us
    select_n x14, other arithmetic, step(): jnp.where(position < mine, new, old)  16.4 us
    dot_general x2, matrix products, shards(): jnp.dot(normalized_output.reshape(-1, width), qkv_weight[layer], preferre...  15.6 us
    slice x4, local copies, waits for them, and re-layouts, shards(): proj[:, :, 2 * width:].astype(jnp.bfloat16)  11.2 us
    convert_element_type x2, other arithmetic, shards(): key = (feature(proj[:, :, width:2 * width]) * flag_f).astype(jnp.bfloat16...  10.2 us
    dynamic_update_slice x8, other arithmetic, shards(): last_state, local_states = lax.scan(advance, start, (kv, persist_factor))  9.48 us
  transfers between devices with their start and end apart: 4, of which 4 were waited for; matrix products, arithmetic and copies ran while one was open for 2% of the time, Pallas kernels for 0%

commit v1 on v0

v1 whole, which is shorter than its diff:
```python
import functools

import jax
import jax.numpy as jnp
from jax import lax
from jax.experimental import pallas as pl
from jax.experimental.pallas import tpu as pltpu
from jax.sharding import PartitionSpec as P

HEADS = 16
HEAD = 64
LAYERS = 2
COLS = 256
MESH = pl.DeviceIdType.MESH


def feature(u):
    return jnp.where(u > 0.0, u + 1.0, jnp.exp(jnp.minimum(u, 0.0)))


def kernel(
    shards, spans, dates,
    frames, mask, wqkv, wout, gain, hscale, tbl, out,
    wbuf, nb, qb, mb, maskb, kb, vb, part, lst, rs_send, rs_recv, dsend, drecv, sb, tks,
    fsem, wsem, rs_ss, rs_rs, d_ss, d_rs, ag_ss, ag_rs, tk_ss, tk_rs,
):
    tokens, width = out.shape
    here = tokens // dates
    groups = width // COLS
    rows = HEAD // shards
    me_s, me_d = lax.axis_index("space"), lax.axis_index("date")

    def peer(off):
        return lax.rem(me_s + off, shards)

    barrier = pltpu.get_barrier_semaphore()
    for off in range(1, shards):
        pl.semaphore_signal(barrier, inc=1, device_id={"space": peer(off)}, device_id_type=MESH)
    for off in range(1, spans):
        pl.semaphore_signal(
            barrier, inc=1, device_id={"date": lax.rem(me_d + off, spans)}, device_id_type=MESH
        )

    def frame_copy():
        return pltpu.make_async_copy(frames, out, fsem)

    def qkv_copy(l, c):
        cols = pl.ds(pl.multiple_of(c * COLS, COLS), COLS)
        return pltpu.make_async_copy(wqkv.at[l, :, cols], wbuf.at[l, c], wsem.at[l, c])

    def out_copy(l, c):
        cols = pl.ds(pl.multiple_of(c * COLS, COLS), COLS)
        slot = c + 3 * groups
        return pltpu.make_async_copy(wout.at[l, :, cols], wbuf.at[l, slot], wsem.at[l, slot])

    frame_copy().start()
    for l in range(LAYERS):
        for g in range(groups):
            qkv_copy(l, groups + g).start()
            qkv_copy(l, 2 * groups + g).start()
        for g in range(groups):
            qkv_copy(l, g).start()
        for g in range(groups):
            out_copy(l, g).start()

    flags = mask[...].astype(jnp.float32)
    for t in range(dates):
        pick = lax.broadcasted_iota(jnp.int32, (dates, COLS), 0) == t
        maskb[pl.ds(t * here, here), :] = lax.dot_general(
            flags, jnp.where(pick, 1.0, 0.0), (((0,), (0,)), ((), ())),
            preferred_element_type=jnp.float32,
        )

    pl.semaphore_wait(barrier, shards + spans - 2)

    def tk_copy(j):
        return pltpu.make_async_remote_copy(
            src_ref=tbl.at[8:16], dst_ref=tks.at[me_d], send_sem=tk_ss.at[j],
            recv_sem=tk_rs.at[me_d], device_id={"date": j}, device_id_type=MESH,
        )

    def tk_arrival(j):
        return pltpu.make_async_remote_copy(
            src_ref=tbl.at[8:16], dst_ref=tks.at[j], send_sem=tk_ss.at[j],
            recv_sem=tk_rs.at[j], device_id={"date": j}, device_id_type=MESH,
        )

    def rs_copy(l, g, p, slot):
        return pltpu.make_async_remote_copy(
            src_ref=rs_send.at[l, g, p], dst_ref=rs_recv.at[l, g, slot],
            send_sem=rs_ss.at[l, g, p], recv_sem=rs_rs.at[l, g, slot],
            device_id={"space": p}, device_id_type=MESH,
        )

    def d_copy(l, g, j, slot):
        return pltpu.make_async_remote_copy(
            src_ref=dsend.at[l, g], dst_ref=drecv.at[l, g, slot],
            send_sem=d_ss.at[l, g, j], recv_sem=d_rs.at[l, g, slot],
            device_id={"date": j}, device_id_type=MESH,
        )

    def ag_copy(l, g, p, slot):
        return pltpu.make_async_remote_copy(
            src_ref=sb.at[l, g, slot], dst_ref=sb.at[l, g, slot],
            send_sem=ag_ss.at[l, g, p], recv_sem=ag_rs.at[l, g, slot],
            device_id={"space": p}, device_id_type=MESH,
        )

    def later(f):
        def body(j, c):
            f(j)
            return c

        lax.fori_loop(me_d + 1, spans, body, 0)

    later(lambda j: tk_copy(j).start())
    frame_copy().wait()

    def columns(g):
        return pl.ds(pl.multiple_of(g * COLS, COLS), COLS)

    def by_layer(ref, l, first, second, cols):
        return jnp.where(l == 0, ref[first : first + 1, cols], ref[second : second + 1, cols])

    def norm(l):
        scale = jnp.where(l == 0, gain[0:1, :], gain[1:2, :])

        def body(t, c):
            at = pl.ds(pl.multiple_of(t * 64, 64), 64)
            xf = out[at, :].astype(jnp.float32)
            msq = jnp.mean(xf * xf, -1, keepdims=True) + 1e-05
            nb[at, :] = (xf * lax.rsqrt(msq) * scale).astype(jnp.bfloat16)
            return c

        lax.fori_loop(0, tokens // 64, body, 0)

    def keys(l, g):
        qkv_copy(l, groups + g).wait()
        qkv_copy(l, 2 * groups + g).wait()
        k = jnp.dot(nb[...], wbuf[l, groups + g], preferred_element_type=jnp.float32)
        kb[...] = (feature(k) * maskb[...]).astype(jnp.bfloat16)
        vb[...] = jnp.dot(
            nb[...], wbuf[l, 2 * groups + g], preferred_element_type=jnp.float32
        ).astype(jnp.bfloat16)
        head = lax.broadcasted_iota(jnp.int32, (HEAD, COLS), 1) // HEAD
        for t in range(dates):
            at = pl.ds(t * here, here)
            pair = lax.dot_general(
                kb[at, :], vb[at, :], (((0,), (0,)), ((), ())), preferred_element_type=jnp.float32
            )
            small = jnp.zeros((HEAD, COLS), jnp.float32)
            for h in range(COLS // HEAD):
                small = jnp.where(head == h, pair[h * HEAD : (h + 1) * HEAD, :], small)
            for r in range(shards):
                part[g, r, pl.ds(t * rows, rows), :] = small[r * rows : (r + 1) * rows, :]
        for r in range(shards):
            rs_send[l, g, r] = part[g, r].astype(jnp.bfloat16)
        for off in range(1, shards):
            rs_copy(l, g, peer(off), me_s).start()

    def queries(l, g):
        qkv_copy(l, g).wait()
        q = jnp.dot(nb[...], wbuf[l, g], preferred_element_type=jnp.float32)
        qb[g] = feature(q).astype(jnp.bfloat16)

    def decays(l, g, t):
        return by_layer(tbl, l, t, dates + t, columns(g))

    def summed(l, g):
        total = part[g, me_s]
        for off in range(1, shards):
            p = peer(off)
            rs_copy(l, g, p, p).wait_recv()
            total = total + rs_recv[l, g, p].astype(jnp.float32)
        state = jnp.zeros((rows, COLS), jnp.float32)
        for t in range(dates):
            state = decays(l, g, t) * state + total[t * rows : (t + 1) * rows, :]
            lst[g, pl.ds(t * rows, rows), :] = state
        dsend[l, g] = state.astype(dsend.dtype)
        later(lambda j: d_copy(l, g, j, me_d).start())

    def joined(l, g):
        @pl.when((l == 0) & (g == 0))
        def _():
            def arrive(j, c):
                tk_arrival(j).wait_recv()
                return c

            lax.fori_loop(0, me_d, arrive, 0)

        def earlier(j, carry):
            d_copy(l, g, j, j).wait_recv()
            kept = jnp.where(l == 0, tks[j, 0:1, columns(g)], tks[j, 1:2, columns(g)])
            return kept * carry + drecv[l, g, j].astype(jnp.float32)

        carry = lax.fori_loop(0, me_d, earlier, jnp.zeros((rows, COLS), jnp.float32))
        states = []
        for t in range(dates):
            carry = decays(l, g, t) * carry
            states.append(lst[g, pl.ds(t * rows, rows), :] + carry)
        sb[l, g, me_s] = jnp.concatenate(states, 0).astype(jnp.bfloat16)
        for off in range(1, shards):
            ag_copy(l, g, peer(off), me_s).start()

    def mix(l, g):
        for off in range(1, shards):
            p = peer(off)
            ag_copy(l, g, p, p).wait_recv()
        blocks = [sb[l, g, r].astype(jnp.float32) for r in range(shards)]
        head = lax.broadcasted_iota(jnp.int32, (HEAD, COLS), 1) // HEAD
        wide = lax.broadcasted_iota(jnp.int32, (COLS, COLS), 1) // HEAD
        tall = lax.broadcasted_iota(jnp.int32, (COLS, COLS), 0) // HEAD
        ones = jnp.where(wide == tall, 1.0, 0.0).astype(jnp.bfloat16)
        scale = by_layer(hscale, l, 0, 1, columns(g))
        for t in range(dates):
            small = jnp.concatenate([b[t * rows : (t + 1) * rows, :] for b in blocks], 0)
            big = jnp.concatenate(
                [jnp.where(head == h, small, 0.0) for h in range(COLS // HEAD)], 0
            ).astype(jnp.bfloat16)
            numer = jnp.dot(
                qb[g, pl.ds(t * here, here), :], big, preferred_element_type=jnp.float32
            )
            msq = jnp.dot(
                (numer * numer).astype(jnp.bfloat16), ones, preferred_element_type=jnp.float32
            )
            msq = msq * (1.0 / HEAD) + 1e-05
            mb[pl.ds(t * here, here), columns(g)] = (numer * lax.rsqrt(msq) * scale).astype(
                jnp.bfloat16
            )

    def project(l, c):
        out_copy(l, c).wait()
        update = jnp.dot(mb[...], wbuf[l, 3 * groups + c], preferred_element_type=jnp.float32)
        at = columns(c)
        out[:, at] = (out[:, at].astype(jnp.float32) + update).astype(jnp.bfloat16)

    def layer(l, c0):
        norm(l)

        def step(s, c):
            @pl.when(s < groups)
            def _():
                keys(l, s)

            @pl.when(s >= groups)
            def _():
                queries(l, s - groups)

            @pl.when((s >= 1) & (s < groups + 1))
            def _():
                summed(l, s - 1)

            @pl.when((s >= 3) & (s < groups + 3))
            def _():
                joined(l, s - 3)

            return c

        lax.fori_loop(0, 2 * groups, step, 0)

        def mix_step(g, c):
            mix(l, g)
            return c

        lax.fori_loop(0, groups, mix_step, 0)

        def project_step(g, c):
            project(l, g)
            return c

        lax.fori_loop(0, groups, project_step, 0)
        return c0

    lax.fori_loop(0, LAYERS, layer, 0)

    later(lambda j: tk_copy(j).wait_send())

    def drain(i, c):
        l, g = i // groups, lax.rem(i, groups)
        for off in range(1, shards):
            rs_copy(l, g, peer(off), me_s).wait_send()
            ag_copy(l, g, peer(off), me_s).wait_send()
        later(lambda j: d_copy(l, g, j, me_d).wait_send())
        return c

    lax.fori_loop(0, LAYERS * groups, drain, 0)


def local(shards, spans, frames, cloud_mask, qkv_weight, out_weight, norm_gain, head_norm_scale, decay):
    dates, here, width = frames.shape
    tokens = dates * here
    groups = width // COLS
    rows = HEAD // shards
    wire = jnp.bfloat16 if rows % 16 == 0 else jnp.float32
    wide = jnp.repeat(decay, HEAD, axis=2)
    kept = jnp.prod(wide, axis=1)
    tbl = jnp.concatenate(
        [wide.reshape(LAYERS * dates, width), kept, jnp.zeros((6, width), jnp.float32)], 0
    )
    vmem = pl.BlockSpec(memory_space=pltpu.VMEM)
    hbm = pl.BlockSpec(memory_space=pl.ANY)
    bf16, f32 = jnp.bfloat16, jnp.float32
    block = (shards, dates * rows, COLS)
    dma = pltpu.SemaphoreType.DMA
    out = pl.pallas_call(
        functools.partial(kernel, shards, spans, dates),
        out_shape=jax.ShapeDtypeStruct((tokens, width), bf16),
        in_specs=[hbm, vmem, hbm, hbm, vmem, vmem, vmem],
        out_specs=vmem,
        scratch_shapes=[
            pltpu.VMEM((LAYERS, 4 * groups, width, COLS), bf16),
            pltpu.VMEM((tokens, width), bf16),
            pltpu.VMEM((groups, tokens, COLS), bf16),
            pltpu.VMEM((tokens, width), bf16),
            pltpu.VMEM((tokens, COLS), f32),
            pltpu.VMEM((tokens, COLS), bf16),
            pltpu.VMEM((tokens, COLS), bf16),
            pltpu.VMEM((groups,) + block, f32),
            pltpu.VMEM((groups, dates * rows, COLS), f32),
            pltpu.VMEM((LAYERS, groups) + block, bf16),
            pltpu.VMEM((LAYERS, groups) + block, bf16),
            pltpu.VMEM((LAYERS, groups, rows, COLS), wire),
            pltpu.VMEM((LAYERS, groups, spans, rows, COLS), wire),
            pltpu.VMEM((LAYERS, groups) + block, bf16),
            pltpu.VMEM((spans, 8, width), f32),
            dma,
            dma((LAYERS, 4 * groups)),
            dma((LAYERS, groups, shards)),
            dma((LAYERS, groups, shards)),
            dma((LAYERS, groups, spans)),
            dma((LAYERS, groups, spans)),
            dma((LAYERS, groups, shards)),
            dma((LAYERS, groups, shards)),
            dma((spans,)),
            dma((spans,)),
        ],
        compiler_params=pltpu.CompilerParams(
            collective_id=0, has_side_effects=True, vmem_limit_bytes=56 * 2**20
        ),
    )(
        frames.reshape(tokens, width), cloud_mask, qkv_weight, out_weight,
        norm_gain, head_norm_scale, tbl,
    )
    return out.reshape(frames.shape)


def solution(mesh):
    placed = (
        P("date", "space", None),
        P("date", "space"),
        P(),
        P(),
        P(),
        P(),
        P(None, "date", None),
    )
    return jax.shard_map(
        functools.partial(local, mesh.shape["space"], mesh.shape["date"]),
        mesh=mesh,
        in_specs=placed,
        out_specs=P("date", "space", None),
        check_vma=False,
    )
```

time: 365 us -> 65 us (0.18)
  waiting for transfers between devices: 203 us -> 0 us
  Pallas kernels: 0 us -> 59.1 us
  blocking collectives: 41.3 us -> 0 us
  other arithmetic: 39.3 us -> 1.41 us
  matrix products: 34.5 us -> 0 us
  local copies, waits for them, and re-layouts: 30.8 us -> 4.16 us
  between operations: 13.5 us -> 0.01 us
    psum x2 -> x0, waiting for transfers between devices: 103 us -> none  [shards(): kv = lax.psum(pairing_partial, 'space')]
    all_gather x2 -> x0, waiting for transfers between devices: 99.3 us -> none  [carried_in(): pieces = jax.tree.map(lambda part: lax.all_gather(part, axis), value)]
    pallas_call x0 -> x1, Pallas kernels: none -> 59.1 us  [local(): pl.pallas_call(functools.partial(kernel, shards, spans, dates), out_shape...]
    all_gather x2 -> x0, blocking collectives: 41.3 us -> none  [carried_in(): pieces = jax.tree.map(lambda part: lax.all_gather(part, axis), value)]
    dot_general x8 -> x0, matrix products: 34.5 us -> none  [the longest x2 15.6 us: shards(): jnp.dot(normalized_output.reshape(-1, width), qkv_weight[layer], preferre...]
    select_n x14 -> x0, other arithmetic: 16.4 us -> none  [step(): jnp.where(position < mine, new, old)]
    slice x6 -> x0, local copies, waits for them, and re-layouts: 12.1 us -> none  [the longest x4 11.2 us: shards(): proj[:, :, 2 * width:].astype(jnp.bfloat16)]
    convert_element_type x4 -> x0, local copies, waits for them, and re-layouts: 11.4 us -> none  [the longest x2 5.71 us: shards(): query = feature(proj[:, :, :width]).astype(jnp.bfloat16).reshape(dates_he...]
  transfers between devices with their start and end apart: 4 -> 0, of which waited for: 4 -> 0; matrix products, arithmetic and copies ran while one was open for 2% -> 0% of each run, Pallas kernels for 0% -> 0%
where the time goes in v1:
time: 65 us; the launch traced here: 64.7 us
  Pallas kernels  59.1 us (91%)
  local copies, waits for them, and re-layouts  4.16 us (6%)
  other arithmetic  1.41 us (2%)
    pallas_call x1, Pallas kernels, local(): pl.pallas_call(functools.partial(kernel, shards, spans, dates), out_shape...  59.1 us
    unnamed x1, local copies, waits for them, and re-layouts  3.08 us

profile of v1, /device:TPU:0, one launch (start us, length us, event | category | flops | bytes accessed | tf_op | source)
XLA Modules:
  0.0 64.7 jit_solution(2940788736363097554)
XLA Ops:
  0.0 0.1 pad.2.clone
  0.1 0.7 %reduce_prod.13 = f32[2,16]{1,0:T(2,128)S(1)} reduce(f32[2,4,16]{2,1,0:T(4,128)} %param.13, f32[]{:T(128)} %constant.0.clone.1), dimensions={1}, to_apply=%region_0.0 | reduce | flops 96 | bytes 644 | tf_op jit(solution)/shard_map/reduce_prod | solution.py:296
  0.8 0.1 reduce_prod.14
  0.9 0.1 reduce_prod.15
  0.9 0.8 %broadcast_in_dim.6 = f32[2,4,16,64]{3,2,1,0:T(8,128)S(1)} broadcast(f32[2,4,16]{2,1,0:T(4,128)} %param.13), dimensions={0,1,2} | broadcast | bytes 33280 | tf_op jit(solution)/shard_map/broadcast_in_dim | solution.py:295
  1.7 0.1 reshape_reshape.3
  1.8 0.7 %maximum_maximum_fusion.tbl = f32[16,1024]{1,0:T(8,128)} fusion(f32[2,1024]{1,0:T(2,128)S(1)} %reduce_prod.15, f32[8,1024]{1,0:T(8,128)S(1)} %reshape_reshape.3, f32[16]{0:T(128)S(1)} %pad.2.clone), kind=kLoop, calls=%fused_computation | loop fusion | flops 32768 | bytes 106560 | tf_op jit(solution)/shard_map/concatenate | solution.py:297
  2.5 59.1 %shard_map.73 = bf16[1024,1024]{1,0:T(8,128)(2,1)} custom-call(bf16[1024,1024]{1,0:T(8,128)(2,1)} %bitcast.5, s32[4,256]{1,0:T(4,128)} %mask.1, bf16[2,1024,3072]{2,1,0:T(8,128)(2,1)} %wqkv.1, bf16[2,1024,1024]{2,1,0:T(8,128)(2,1)} %wout.1, f32[2,1024]{1,0:T(2,128)} %gain.1, f32[2,1024]{1,0:T(2,128)} %hscale.1, f32[16,1024]{1,0:T(8,128)} %maximum_maximum_fusion.tbl), custom_call_target="tpu_custom_call" | custom-call | tf_op jit(solution)/shard_map/pallas_call | solution.py:305
  61.6 3.1 %copy.9 = bf16[4,256,1024]{2,1,0:T(8,128)(2,1)} copy(bf16[4,256,1024]{2,1,0:T(8,128)(2,1)} %bitcast.4) | data formatting | bytes 4194304
  (1 shorter events, 0.0 us)

commit v2 on v1

--- a/solution.py
+++ b/solution.py
@@ -11,6 +11,7 @@
 HEAD = 64
 LAYERS = 2
 COLS = 256
+PIECES = 8
 MESH = pl.DeviceIdType.MESH
 
 
@@ -20,8 +21,8 @@
 
 def kernel(
     shards, spans, dates,
-    frames, mask, wqkv, wout, gain, hscale, tbl, out,
-    wbuf, nb, qb, mb, maskb, kb, vb, part, lst, rs_send, rs_recv, dsend, drecv, sb, tks,
+    frames, mask, wqkv, wout, gain, hscale, decay, out,
+    tbl, wbuf, nb, qb, mb, maskb, kb, vb, part, lst, rs_send, rs_recv, dsend, drecv, sb, tks,
     fsem, wsem, rs_ss, rs_rs, d_ss, d_rs, ag_ss, ag_rs, tk_ss, tk_rs,
 ):
     tokens, width = out.shape
@@ -71,6 +72,22 @@
             preferred_element_type=jnp.float32,
         )
 
+    spread = jnp.where(
+        lax.broadcasted_iota(jnp.int32, (HEADS, width), 1) // HEAD
+        == lax.broadcasted_iota(jnp.int32, (HEADS, width), 0), 1.0, 0.0,
+    )
+    tail = []
+    for l in range(LAYERS):
+        kept_l = jnp.dot(
+            decay[l], spread, precision=lax.Precision.HIGHEST, preferred_element_type=jnp.float32
+        )
+        tbl[pl.ds(l * dates, dates), :] = kept_l
+        whole = kept_l[0:1, :]
+        for t in range(1, dates):
+            whole = whole * kept_l[t : t + 1, :]
+        tail.append(whole)
+    tbl[8:16, :] = jnp.concatenate(tail + [jnp.zeros((8 - LAYERS, width), jnp.float32)], 0)
+
     pl.semaphore_wait(barrier, shards + spans - 2)
 
     def tk_copy(j):
@@ -126,13 +143,13 @@
         scale = jnp.where(l == 0, gain[0:1, :], gain[1:2, :])
 
         def body(t, c):
-            at = pl.ds(pl.multiple_of(t * 64, 64), 64)
+            at = pl.ds(pl.multiple_of(t * COLS, COLS), COLS)
             xf = out[at, :].astype(jnp.float32)
             msq = jnp.mean(xf * xf, -1, keepdims=True) + 1e-05
             nb[at, :] = (xf * lax.rsqrt(msq) * scale).astype(jnp.bfloat16)
             return c
 
-        lax.fori_loop(0, tokens // 64, body, 0)
+        lax.fori_loop(0, tokens // COLS, body, 0)
 
     def keys(l, g):
         qkv_copy(l, groups + g).wait()
@@ -246,13 +263,13 @@
             def _():
                 queries(l, s - groups)
 
-            @pl.when((s >= 1) & (s < groups + 1))
+            @pl.when((s >= 2) & (s < groups + 2))
             def _():
-                summed(l, s - 1)
-
-            @pl.when((s >= 3) & (s < groups + 3))
+                summed(l, s - 2)
+
+            @pl.when(s >= groups)
             def _():
-                joined(l, s - 3)
+                joined(l, s - groups)
 
             return c
 
@@ -284,6 +301,18 @@
         return c
 
     lax.fori_loop(0, LAYERS * groups, drain, 0)
+
+
+def hand_over(src, dst, sems):
+    step = src.shape[0] // PIECES
+    copies = [
+        pltpu.make_async_copy(src.at[pl.ds(i * step, step)], dst.at[pl.ds(i * step, step)], sems.at[i])
+        for i in range(PIECES)
+    ]
+    for copy in copies:
+        copy.start()
+    for copy in copies:
+        copy.wait()
 
 
 def local(shards, spans, frames, cloud_mask, qkv_weight, out_weight, norm_gain, head_norm_scale, decay):
@@ -292,11 +321,6 @@
     groups = width // COLS
     rows = HEAD // shards
     wire = jnp.bfloat16 if rows % 16 == 0 else jnp.float32
-    wide = jnp.repeat(decay, HEAD, axis=2)
-    kept = jnp.prod(wide, axis=1)
-    tbl = jnp.concatenate(
-        [wide.reshape(LAYERS * dates, width), kept, jnp.zeros((6, width), jnp.float32)], 0
-    )
     vmem = pl.BlockSpec(memory_space=pltpu.VMEM)
     hbm = pl.BlockSpec(memory_space=pl.ANY)
     bf16, f32 = jnp.bfloat16, jnp.float32
@@ -308,6 +332,7 @@
         in_specs=[hbm, vmem, hbm, hbm, vmem, vmem, vmem],
         out_specs=vmem,
         scratch_shapes=[
+            pltpu.VMEM((16, width), f32),
             pltpu.VMEM((LAYERS, 4 * groups, width, COLS), bf16),
             pltpu.VMEM((tokens, width), bf16),
             pltpu.VMEM((groups, tokens, COLS), bf16),
@@ -339,9 +364,16 @@
         ),
     )(
         frames.reshape(tokens, width), cloud_mask, qkv_weight, out_weight,
-        norm_gain, head_norm_scale, tbl,
+        norm_gain, head_norm_scale, decay,
     )
-    return out.reshape(frames.shape)
+    result = pl.pallas_call(
+        hand_over,
+        out_shape=jax.ShapeDtypeStruct((tokens, width), bf16),
+        in_specs=[hbm],
+        out_specs=hbm,
+        scratch_shapes=[dma((PIECES,))],
+    )(out)
+    return result.reshape(frames.shape)
 
 
 def solution(mesh):

time: 65 us -> 119 us (1.83)
  Pallas kernels: 59.1 us -> 119 us
  local copies, waits for them, and re-layouts: 4.16 us -> 0 us
  other arithmetic: 1.41 us -> 0 us
    pallas_call x0 -> x1, Pallas kernels: none -> 64.7 us  [local(): pl.pallas_call(hand_over, out_shape=jax.ShapeDtypeStruct((tokens, width),...]
    pallas_call x1, Pallas kernels: 59.1 us -> 53.9 us  [local(): pl.pallas_call(functools.partial(kernel, shards, spans, dates), out_shape...]
    unnamed x1 -> x0, local copies, waits for them, and re-layouts: 3.08 us -> none
where the time goes in v2:
time: 119 us
  Pallas kernels  119 us (100%)
    pallas_call x1, Pallas kernels, local(): pl.pallas_call(hand_over, out_shape=jax.ShapeDtypeStruct((tokens, width),...  64.7 us
    pallas_call x1, Pallas kernels, local(): pl.pallas_call(functools.partial(kernel, shards, spans, dates), out_shape...  53.9 us

profile of v2, /device:TPU:0, one launch (start us, length us, event | category | flops | bytes accessed | tf_op | source)
XLA Modules:
  0.0 118.6 jit_solution(4350044133014787013)
XLA Ops:
  0.0 53.9 %shard_map.73.src = bf16[1024,1024]{1,0:T(8,128)(2,1)} custom-call(bf16[1024,1024]{1,0:T(8,128)(2,1)} %bitcast.2, s32[4,256]{1,0:T(4,128)} %mask.1, bf16[2,1024,3072]{2,1,0:T(8,128)(2,1)} %wqkv.1, bf16[2,1024,1024]{2,1,0:T(8,128)(2,1)} %wout.1, f32[2,1024]{1,0:T(2,128)} %gain.1, f32[2,1024]{1,0:T(2,128)} %hscale.1, f32[2,4,16]{2,1,0:T(4,128)} %decay.1), custom_call_target="tpu_custom_call" | custom-call | tf_op jit(solution)/shard_map/pallas_call | solution.py:329
  53.9 64.7 %shard_map.74 = bf16[1024,1024]{1,0:T(8,128)(2,1)} custom-call(bf16[1024,1024]{1,0:T(8,128)(2,1)} %shard_map.73.src), custom_call_target="tpu_custom_call" | custom-call | tf_op jit(solution)/shard_map/pallas_call | solution.py:369

commit v3 on v2

--- a/solution.py
+++ b/solution.py
@@ -11,7 +11,6 @@
 HEAD = 64
 LAYERS = 2
 COLS = 256
-PIECES = 8
 MESH = pl.DeviceIdType.MESH
 
 
@@ -301,18 +300,6 @@
         return c
 
     lax.fori_loop(0, LAYERS * groups, drain, 0)
-
-
-def hand_over(src, dst, sems):
-    step = src.shape[0] // PIECES
-    copies = [
-        pltpu.make_async_copy(src.at[pl.ds(i * step, step)], dst.at[pl.ds(i * step, step)], sems.at[i])
-        for i in range(PIECES)
-    ]
-    for copy in copies:
-        copy.start()
-    for copy in copies:
-        copy.wait()
 
 
 def local(shards, spans, frames, cloud_mask, qkv_weight, out_weight, norm_gain, head_norm_scale, decay):
@@ -366,14 +353,7 @@
         frames.reshape(tokens, width), cloud_mask, qkv_weight, out_weight,
         norm_gain, head_norm_scale, decay,
     )
-    result = pl.pallas_call(
-        hand_over,
-        out_shape=jax.ShapeDtypeStruct((tokens, width), bf16),
-        in_specs=[hbm],
-        out_specs=hbm,
-        scratch_shapes=[dma((PIECES,))],
-    )(out)
-    return result.reshape(frames.shape)
+    return out.reshape(frames.shape)
 
 
 def solution(mesh):

time: 119 us -> 57.2 us (0.48)
  Pallas kernels: 119 us -> 53.9 us
  local copies, waits for them, and re-layouts: 0 us -> 3.08 us
    pallas_call x1 -> x0, Pallas kernels: 64.7 us -> none  [local(): pl.pallas_call(hand_over, out_shape=jax.ShapeDtypeStruct((tokens, width),...]
    unnamed x0 -> x1, local copies, waits for them, and re-layouts: none -> 3.08 us
where the time goes in v3:
time: 57.2 us; the launch traced here: 57 us
  Pallas kernels  53.9 us (94%)
  local copies, waits for them, and re-layouts  3.08 us (5%)
    pallas_call x1, Pallas kernels, local(): pl.pallas_call(functools.partial(kernel, shards, spans, dates), out_shape...  53.9 us
    unnamed x1, local copies, waits for them, and re-layouts  3.08 us

profile of v3, /device:TPU:0, one launch (start us, length us, event | category | flops | bytes accessed | tf_op | source)
XLA Modules:
  0.0 57.0 jit_solution(11842364140573930620)
XLA Ops:
  0.0 53.9 %shard_map.73 = bf16[1024,1024]{1,0:T(8,128)(2,1)} custom-call(bf16[1024,1024]{1,0:T(8,128)(2,1)} %bitcast.3, s32[4,256]{1,0:T(4,128)} %mask.1, bf16[2,1024,3072]{2,1,0:T(8,128)(2,1)} %wqkv.1, bf16[2,1024,1024]{2,1,0:T(8,128)(2,1)} %wout.1, f32[2,1024]{1,0:T(2,128)} %gain.1, f32[2,1024]{1,0:T(2,128)} %hscale.1, f32[2,4,16]{2,1,0:T(4,128)} %decay.1), custom_call_target="tpu_custom_call" | custom-call | tf_op jit(solution)/shard_map/pallas_call | solution.py:316
  53.9 3.1 %copy.9 = bf16[4,256,1024]{2,1,0:T(8,128)(2,1)} copy(bf16[4,256,1024]{2,1,0:T(8,128)(2,1)} %bitcast.2) | data formatting | bytes 4194304

commit v4 on v3

--- a/solution.py
+++ b/solution.py
@@ -21,8 +21,8 @@
 def kernel(
     shards, spans, dates,
     frames, mask, wqkv, wout, gain, hscale, decay, out,
-    tbl, wbuf, nb, qb, mb, maskb, kb, vb, part, lst, rs_send, rs_recv, dsend, drecv, sb, tks,
-    fsem, wsem, rs_ss, rs_rs, d_ss, d_rs, ag_ss, ag_rs, tk_ss, tk_rs,
+    tbl, wbuf, nb, qb, mb, maskb, kb, vb, acc, part, own, lst, rs_send, rs_recv, y_send, y_recv, dsend, drecv, sb, tks,
+    fsem, wsem, p_ss, p_rs, y_ss, y_rs, d_ss, d_rs, ag_ss, ag_rs, fw_ss, tk_ss, tk_rs,
 ):
     tokens, width = out.shape
     here = tokens // dates
@@ -30,12 +30,18 @@
     rows = HEAD // shards
     me_s, me_d = lax.axis_index("space"), lax.axis_index("date")
 
-    def peer(off):
-        return lax.rem(me_s + off, shards)
+    lines, line, core = shards // 2, me_s // 2, lax.rem(me_s, 2)
+    mate = me_s + 1 - 2 * core
+
+    def across(off):
+        return lax.rem(line + off, lines)
 
     barrier = pltpu.get_barrier_semaphore()
-    for off in range(1, shards):
-        pl.semaphore_signal(barrier, inc=1, device_id={"space": peer(off)}, device_id_type=MESH)
+    pl.semaphore_signal(barrier, inc=1, device_id={"space": mate}, device_id_type=MESH)
+    for off in range(1, lines):
+        pl.semaphore_signal(
+            barrier, inc=1, device_id={"space": 2 * across(off) + core}, device_id_type=MESH
+        )
     for off in range(1, spans):
         pl.semaphore_signal(
             barrier, inc=1, device_id={"date": lax.rem(me_d + off, spans)}, device_id_type=MESH
@@ -87,7 +93,7 @@
         tail.append(whole)
     tbl[8:16, :] = jnp.concatenate(tail + [jnp.zeros((8 - LAYERS, width), jnp.float32)], 0)
 
-    pl.semaphore_wait(barrier, shards + spans - 2)
+    pl.semaphore_wait(barrier, lines + spans - 1)
 
     def tk_copy(j):
         return pltpu.make_async_remote_copy(
@@ -101,11 +107,25 @@
             recv_sem=tk_rs.at[j], device_id={"date": j}, device_id_type=MESH,
         )
 
-    def rs_copy(l, g, p, slot):
-        return pltpu.make_async_remote_copy(
-            src_ref=rs_send.at[l, g, p], dst_ref=rs_recv.at[l, g, slot],
-            send_sem=rs_ss.at[l, g, p], recv_sem=rs_rs.at[l, g, slot],
-            device_id={"space": p}, device_id_type=MESH,
+    def pair_copy(l, g):
+        return pltpu.make_async_remote_copy(
+            src_ref=rs_send.at[l, g], dst_ref=rs_recv.at[l, g],
+            send_sem=p_ss.at[l, g], recv_sem=p_rs.at[l, g],
+            device_id={"space": mate}, device_id_type=MESH,
+        )
+
+    def y_copy(l, g, y, slot):
+        return pltpu.make_async_remote_copy(
+            src_ref=y_send.at[l, g, y], dst_ref=y_recv.at[l, g, slot],
+            send_sem=y_ss.at[l, g, y], recv_sem=y_rs.at[l, g, slot],
+            device_id={"space": 2 * y + core}, device_id_type=MESH,
+        )
+
+    def fw_copy(l, g, slot):
+        return pltpu.make_async_remote_copy(
+            src_ref=sb.at[l, g, slot], dst_ref=sb.at[l, g, slot],
+            send_sem=fw_ss.at[l, g, slot], recv_sem=ag_rs.at[l, g, slot],
+            device_id={"space": mate}, device_id_type=MESH,
         )
 
     def d_copy(l, g, j, slot):
@@ -168,11 +188,19 @@
             for h in range(COLS // HEAD):
                 small = jnp.where(head == h, pair[h * HEAD : (h + 1) * HEAD, :], small)
             for r in range(shards):
-                part[g, r, pl.ds(t * rows, rows), :] = small[r * rows : (r + 1) * rows, :]
-        for r in range(shards):
-            rs_send[l, g, r] = part[g, r].astype(jnp.bfloat16)
-        for off in range(1, shards):
-            rs_copy(l, g, peer(off), me_s).start()
+                part[g, r % 2, r // 2, pl.ds(t * rows, rows), :] = small[r * rows : (r + 1) * rows, :]
+        rs_send[l, g] = part[g, 1 - core].astype(jnp.bfloat16)
+        pair_copy(l, g).start()
+
+    def paired(l, g):
+        pair_copy(l, g).wait_recv()
+        for off in range(1, lines):
+            y = across(off)
+            y_send[l, g, y] = (part[g, core, y] + rs_recv[l, g, y].astype(jnp.float32)).astype(
+                jnp.bfloat16
+            )
+            y_copy(l, g, y, line).start()
+        own[g] = part[g, core, line] + rs_recv[l, g, line].astype(jnp.float32)
 
     def queries(l, g):
         qkv_copy(l, g).wait()
@@ -183,11 +211,11 @@
         return by_layer(tbl, l, t, dates + t, columns(g))
 
     def summed(l, g):
-        total = part[g, me_s]
-        for off in range(1, shards):
-            p = peer(off)
-            rs_copy(l, g, p, p).wait_recv()
-            total = total + rs_recv[l, g, p].astype(jnp.float32)
+        total = own[g]
+        for off in range(1, lines):
+            y = across(off)
+            y_copy(l, g, y, y).wait_recv()
+            total = total + y_recv[l, g, y].astype(jnp.float32)
         state = jnp.zeros((rows, COLS), jnp.float32)
         for t in range(dates):
             state = decays(l, g, t) * state + total[t * rows : (t + 1) * rows, :]
@@ -215,13 +243,20 @@
             carry = decays(l, g, t) * carry
             states.append(lst[g, pl.ds(t * rows, rows), :] + carry)
         sb[l, g, me_s] = jnp.concatenate(states, 0).astype(jnp.bfloat16)
-        for off in range(1, shards):
-            ag_copy(l, g, peer(off), me_s).start()
+        for off in range(1, lines):
+            ag_copy(l, g, 2 * across(off) + core, me_s).start()
+        ag_copy(l, g, mate, me_s).start()
+
+    def forwarded(l, g):
+        for off in range(1, lines):
+            slot = 2 * across(off) + core
+            ag_copy(l, g, slot, slot).wait_recv()
+            fw_copy(l, g, slot).start()
 
     def mix(l, g):
-        for off in range(1, shards):
-            p = peer(off)
-            ag_copy(l, g, p, p).wait_recv()
+        ag_copy(l, g, mate, mate).wait_recv()
+        for off in range(1, lines):
+            fw_copy(l, g, 2 * across(off) + 1 - core).wait_recv()
         blocks = [sb[l, g, r].astype(jnp.float32) for r in range(shards)]
         head = lax.broadcasted_iota(jnp.int32, (HEAD, COLS), 1) // HEAD
         wide = lax.broadcasted_iota(jnp.int32, (COLS, COLS), 1) // HEAD
@@ -244,11 +279,20 @@
                 jnp.bfloat16
             )
 
-    def project(l, c):
+    half = width // 2
+
+    def project_first(l, c):
         out_copy(l, c).wait()
-        update = jnp.dot(mb[...], wbuf[l, 3 * groups + c], preferred_element_type=jnp.float32)
-        at = columns(c)
-        out[:, at] = (out[:, at].astype(jnp.float32) + update).astype(jnp.bfloat16)
+        update = jnp.dot(
+            mb[:, :half], wbuf[l, 3 * groups + c, :half], preferred_element_type=jnp.float32
+        )
+        acc[c] = out[:, columns(c)].astype(jnp.float32) + update
+
+    def project_rest(l, c):
+        update = jnp.dot(
+            mb[:, half:], wbuf[l, 3 * groups + c, half:], preferred_element_type=jnp.float32
+        )
+        out[:, columns(c)] = (acc[c] + update).astype(jnp.bfloat16)
 
     def layer(l, c0):
         norm(l)
@@ -262,6 +306,10 @@
             def _():
                 queries(l, s - groups)
 
+            @pl.when((s >= 1) & (s < groups + 1))
+            def _():
+                paired(l, s - 1)
+
             @pl.when((s >= 2) & (s < groups + 2))
             def _():
                 summed(l, s - 2)
@@ -270,21 +318,26 @@
             def _():
                 joined(l, s - groups)
 
+            @pl.when(s >= groups + 1)
+            def _():
+                forwarded(l, s - groups - 1)
+
             return c
 
         lax.fori_loop(0, 2 * groups, step, 0)
 
-        def mix_step(g, c):
-            mix(l, g)
-            return c
-
-        lax.fori_loop(0, groups, mix_step, 0)
-
-        def project_step(g, c):
-            project(l, g)
-            return c
-
-        lax.fori_loop(0, groups, project_step, 0)
+        def each(first, last, f):
+            def body(i, c):
+                f(l, i)
+                return c
+
+            lax.fori_loop(first, last, body, 0)
+
+        each(0, groups // 2, mix)
+        forwarded(l, groups - 1)
+        each(0, groups, project_first)
+        each(groups // 2, groups, mix)
+        each(0, groups, project_rest)
         return c0
 
     lax.fori_loop(0, LAYERS, layer, 0)
@@ -293,9 +346,12 @@
 
     def drain(i, c):
         l, g = i // groups, lax.rem(i, groups)
-        for off in range(1, shards):
-            rs_copy(l, g, peer(off), me_s).wait_send()
-            ag_copy(l, g, peer(off), me_s).wait_send()
+        pair_copy(l, g).wait_send()
+        ag_copy(l, g, mate, me_s).wait_send()
+        for off in range(1, lines):
+            y_copy(l, g, across(off), line).wait_send()
+            ag_copy(l, g, 2 * across(off) + core, me_s).wait_send()
+            fw_copy(l, g, 2 * across(off) + core).wait_send()
         later(lambda j: d_copy(l, g, j, me_d).wait_send())
         return c
 
@@ -312,6 +368,7 @@
     hbm = pl.BlockSpec(memory_space=pl.ANY)
     bf16, f32 = jnp.bfloat16, jnp.float32
     block = (shards, dates * rows, COLS)
+    split = (shards // 2, dates * rows, COLS)
     dma = pltpu.SemaphoreType.DMA
     out = pl.pallas_call(
         functools.partial(kernel, shards, spans, dates),
@@ -327,20 +384,27 @@
             pltpu.VMEM((tokens, COLS), f32),
             pltpu.VMEM((tokens, COLS), bf16),
             pltpu.VMEM((tokens, COLS), bf16),
-            pltpu.VMEM((groups,) + block, f32),
+            pltpu.VMEM((groups, tokens, COLS), f32),
+            pltpu.VMEM((groups, 2) + split, f32),
             pltpu.VMEM((groups, dates * rows, COLS), f32),
-            pltpu.VMEM((LAYERS, groups) + block, bf16),
-            pltpu.VMEM((LAYERS, groups) + block, bf16),
+            pltpu.VMEM((groups, dates * rows, COLS), f32),
+            pltpu.VMEM((LAYERS, groups) + split, bf16),
+            pltpu.VMEM((LAYERS, groups) + split, bf16),
+            pltpu.VMEM((LAYERS, groups) + split, bf16),
+            pltpu.VMEM((LAYERS, groups) + split, bf16),
             pltpu.VMEM((LAYERS, groups, rows, COLS), wire),
             pltpu.VMEM((LAYERS, groups, spans, rows, COLS), wire),
             pltpu.VMEM((LAYERS, groups) + block, bf16),
             pltpu.VMEM((spans, 8, width), f32),
             dma,
             dma((LAYERS, 4 * groups)),
-            dma((LAYERS, groups, shards)),
-            dma((LAYERS, groups, shards)),
+            dma((LAYERS, groups)),
+            dma((LAYERS, groups)),
+            dma((LAYERS, groups, shards // 2)),
+            dma((LAYERS, groups, shards // 2)),
             dma((LAYERS, groups, spans)),
             dma((LAYERS, groups, spans)),
+            dma((LAYERS, groups, shards)),
             dma((LAYERS, groups, shards)),
             dma((LAYERS, groups, shards)),
             dma((spans,)),

time: 57.2 us -> 64.8 us (1.13)
  Pallas kernels: 53.9 us -> 61.4 us
    pallas_call x1, Pallas kernels: 53.9 us -> 61.4 us  [local(): pl.pallas_call(functools.partial(kernel, shards, spans, dates), out_shape...]
where the time goes in v4:
time: 64.8 us; the launch traced here: 64.5 us
  Pallas kernels  61.4 us (95%)
  local copies, waits for them, and re-layouts  3.08 us (5%)
    pallas_call x1, Pallas kernels, local(): pl.pallas_call(functools.partial(kernel, shards, spans, dates), out_shape...  61.4 us
    unnamed x1, local copies, waits for them, and re-layouts  3.08 us

profile of v4, /device:TPU:0, one launch (start us, length us, event | category | flops | bytes accessed | tf_op | source)
XLA Modules:
  0.0 64.5 jit_solution(2556053613178631731)
XLA Ops:
  0.0 61.4 %shard_map.73 = bf16[1024,1024]{1,0:T(8,128)(2,1)} custom-call(bf16[1024,1024]{1,0:T(8,128)(2,1)} %bitcast.3, s32[4,256]{1,0:T(4,128)} %mask.1, bf16[2,1024,3072]{2,1,0:T(8,128)(2,1)} %wqkv.1, bf16[2,1024,1024]{2,1,0:T(8,128)(2,1)} %wout.1, f32[2,1024]{1,0:T(2,128)} %gain.1, f32[2,1024]{1,0:T(2,128)} %hscale.1, f32[2,4,16]{2,1,0:T(4,128)} %decay.1), custom_call_target="tpu_custom_call" | custom-call | tf_op jit(solution)/shard_map/pallas_call | solution.py:373
  61.4 3.1 %copy.9 = bf16[4,256,1024]{2,1,0:T(8,128)(2,1)} copy(bf16[4,256,1024]{2,1,0:T(8,128)(2,1)} %bitcast.2) | data formatting | bytes 4194304
